TPU v7x, 128 devices: a whole 4x4x4 slice. The times are simulated.
128 devices in a mesh: grp: 64 (over z, y, x), tp: 2 (over core).
Axes of the slice: x: 4, y: 4, z: 4, core: 2. Of those that a mesh axis runs over, the one named last changes fastest.
Arguments:
- context: bfloat16 [65536, 3072], P('grp', 'tp'), may hold values from -6 to 6
- residual: bfloat16 [65536, 6144], P('grp', 'tp')
- out_weight: bfloat16 [3072, 6144], P('tp'), may hold values from -0.15625 to 0.15625
- adapter_down: bfloat16 [3072, 128], P('tp'), may hold values from -0.109375 to 0.109375
- adapter_up: bfloat16 [128, 6144], P(None, 'tp'), may hold values from -0.5 to 0.5
- norm_gain: float32 [6144], P('tp'), may hold values from 0.25 to 1.75
- lengths: int32 [64], P('grp'), may hold values from 1 to 1024
- route_group: int32 [64, 64], P('grp'), may hold values from 0 to 63, as said below
- route_slot: int32 [64, 64], P('grp'), may hold values from 0 to 63, as said below
Outputs:
- policy_rows: bfloat16 [65536, 6144], P('grp', 'tp')
- reference_rows: bfloat16 [65536, 6144], P('grp', 'tp')
Inputs may be any that keep to these rules, and one draw needn't show every extreme that they name: Each row of route_group names every learner group exactly once; the two groups of a chosen and rejected pair have equal rows of route_group. `route_slot`: at each learner group the 64 blocks that arrive, one from each group, take the slots 0 to 63 once each; the two blocks of a pair sit in slots 2q and 2q + 1.
All inputs are finite; a program needn't handle non-finite values.
Results may differ from a plain program's by a relative error of at most 0.012.
Values may be sent and summed in bfloat16 or wider, within the bound.
A program may use at most 192 MiB of HBM per device.

v0:
```python
import jax
import jax.numpy as jnp
from jax import lax
from jax.sharding import PartitionSpec as P

EPSILON = 1e-05


def live_mask(valid_count, block_size):
    token_index = jnp.arange(block_size, dtype=jnp.int32)
    return (token_index[None, :] < valid_count[:, None]).reshape(-1).astype(jnp.float32)


def layer_rows(
    context_rows, residual_rows, valid_count, out_weight, adapter_down, adapter_up, norm_gain
):
    row_count = context_rows.shape[0]
    partial_value = jnp.dot(context_rows, out_weight, preferred_element_type=jnp.float32)
    attention = lax.psum_scatter(
        partial_value.astype(jnp.bfloat16), "tp", scatter_dimension=1, tiled=True
    ).astype(jnp.float32)
    adapter_part = jnp.dot(context_rows, adapter_down, preferred_element_type=jnp.float32)
    adapter_full = lax.psum(adapter_part.astype(jnp.bfloat16), "tp")
    reference_hidden = residual_rows.astype(jnp.float32) + attention
    policy_hidden = reference_hidden + jnp.dot(
        adapter_full, adapter_up, preferred_element_type=jnp.float32
    )
    square_sums = lax.psum(
        (
            jnp.sum(policy_hidden * policy_hidden, axis=1),
            jnp.sum(reference_hidden * reference_hidden, axis=1),
        ),
        "tp",
    )
    full_width = lax.axis_size("tp") * residual_rows.shape[1]
    block_size = row_count // valid_count.shape[0]
    scaled_gain = live_mask(valid_count, block_size)[:, None] * norm_gain[None, :]
    policy_rows = (
        policy_hidden * lax.rsqrt(square_sums[0] / full_width + EPSILON)[:, None] * scaled_gain
    ).astype(jnp.bfloat16)
    reference_rows = (
        reference_hidden * lax.rsqrt(square_sums[1] / full_width + EPSILON)[:, None] * scaled_gain
    ).astype(jnp.bfloat16)
    return (policy_rows, reference_rows)


def local(
    context,
    residual,
    out_weight,
    adapter_down,
    adapter_up,
    norm_gain,
    lengths,
    route_group,
    route_slot,
):
    group_total = lax.axis_size("grp")
    block_size = context.shape[0] // group_total
    position = jnp.arange(group_total, dtype=jnp.int32)
    valid_count = jnp.clip(lengths[0] - position * block_size, 0, block_size)
    send_order = jnp.zeros((group_total,), jnp.int32).at[route_group[0]].set(position)
    seat_sent = route_slot[0][send_order]
    context_width = context.shape[1]
    residual_width = residual.shape[1]
    meta_sent = jnp.stack([seat_sent, valid_count[send_order]], axis=1)
    arrived = (
        lax.all_to_all(
            context.reshape(group_total, block_size, context_width)[send_order],
            "grp",
            split_axis=0,
            concat_axis=0,
            tiled=True,
        ),
        lax.all_to_all(
            residual.reshape(group_total, block_size, residual_width)[send_order],
            "grp",
            split_axis=0,
            concat_axis=0,
            tiled=True,
        ),
        lax.all_to_all(meta_sent, "grp", split_axis=0, concat_axis=0, tiled=True),
    )
    placement = jnp.zeros((group_total,), jnp.int32).at[arrived[2][:, 0]].set(position)
    context_rows = arrived[0][placement].reshape(-1, context_width)
    residual_rows = arrived[1][placement].reshape(-1, residual_width)
    valid_here = arrived[2][placement, 1]
    return layer_rows(
        context_rows, residual_rows, valid_here, out_weight, adapter_down, adapter_up, norm_gain
    )


def solution(mesh):
    in_specs = (
        P("grp", "tp"),
        P("grp", "tp"),
        P("tp", None),
        P("tp", None),
        P(None, "tp"),
        P("tp"),
        P("grp"),
        P("grp", None),
        P("grp", None),
    )
    out_specs = (P("grp", "tp"), P("grp", "tp"))
    return jax.shard_map(local, mesh=mesh, in_specs=in_specs, out_specs=out_specs, check_vma=False)
```

profile of v0, /device:TPU:11, one launch (start us, length us, event | category | flops | bytes accessed | tf_op | source)
XLA Modules:
  0.0 257.8 jit_solution(10259536737532675304)
XLA Ops:
  7.2 0.0 copy-start
  8.0 0.8 fusion.4
  8.8 0.8 scatter_custom_fusion
  9.6 0.8 gather_fusion.2
  10.4 1.4 gather_fusion.1
  11.8 0.7 copy.11
  12.5 10.8 %all-to-all-start.1 = ((s32[64,1,2]{2,1,0:T(1,128)}), s32[64,1,2]{2,1,0:T(1,128)S(1)}, u32[]{:S(2)}, u32[]{:S(2)}) async-start(s32[64,1,2]{2,1,0:T(1,128)} %copy.11), calls=%async_computation.1 | async-start | bytes 65536 | tf_op jit(solution)/shard_map/all_to_all | solution.py:82
  23.4 0.0 copy-done
  23.4 2.4 gather_fusion.4
  25.8 4.3 %all-to-all-done.1 = s32[64,1,2]{2,1,0:T(1,128)S(1)} async-done(((s32[64,1,2]{2,1,0:T(1,128)}), s32[64,1,2]{2,1,0:T(1,128)S(1)}, u32[]{:S(2)}, u32[]{:S(2)}) %all-to-all-start.1) | async-done | bytes 544 | tf_op jit(solution)/shard_map/all_to_all | solution.py:82
  30.1 7.0 %all-to-all-start.2 = ((bf16[64,16,1536]{2,1,0:T(8,128)(2,1)}), bf16[64,16,1536]{2,1,0:T(8,128)(2,1)}, u32[]{:S(2)}, u32[]{:S(2)}) async-start(bf16[64,16,1536]{2,1,0:T(8,128)(2,1)} %gather_fusion.4), calls=%async_computation.2 | async-start | bytes 6291456 | tf_op jit(solution)/shard_map/all_to_all | solution.py:68
  37.1 0.0 reduce-scatter.2.cloned.1.call-start
  37.2 0.1 copy.12
  37.3 0.8 scatter_custom_fusion.1
  38.1 36.8 %all-to-all-done.2 = bf16[64,16,1536]{2,1,0:T(8,128)(2,1)} async-done(((bf16[64,16,1536]{2,1,0:T(8,128)(2,1)}), bf16[64,16,1536]{2,1,0:T(8,128)(2,1)}, u32[]{:S(2)}, u32[]{:S(2)}) %all-to-all-start.2) | async-done | bytes 3145760 | tf_op jit(solution)/shard_map/all_to_all | solution.py:68
  74.8 4.3 %gather_fusion.5 = bf16[64,16,1536]{2,1,0:T(8,128)(2,1)} fusion(bf16[64,16,1536]{2,1,0:T(8,128)(2,1)} %all-to-all-done.2, s32[1024]{0:T(1024)S(1)} %pad_clamp_fusion), kind=kCustom, calls=%fused_computation.5 | custom fusion | bytes 6291712 | tf_op jit(solution)/shard_map/gather | solution.py:85
  79.1 25.8 %convolution_convert_fusion = bf16[1024,6144]{1,0:T(8,128)(2,1)} fusion(bf16[1024,1536]{1,0:T(8,128)(2,1)} %bitcast.35, bf16[1536,6144]{1,0:T(8,128)(2,1)} %param.11), kind=kOutput, calls=%fused_computation.16 | convolution fusion | flops 19333644288 | bytes 34603008 | tf_op jit(solution)/shard_map/dot_general | solution.py:18
  104.9 0.0 reduce-scatter.2.cloned.1.call-update
  104.9 6.4 %gather_fusion = bf16[64,16,3072]{2,1,0:T(8,128)(2,1)} fusion(bf16[64,16,3072]{2,1,0:T(8,128)(2,1)} %bitcast.34, s32[1024]{0:T(1024)S(1)} %pad_clamp_fusion.1), kind=kCustom, calls=%fused_computation | custom fusion | bytes 12583168 | tf_op jit(solution)/shard_map/gather | solution.py:76
  111.4 0.0 copy-start.4
  111.4 11.1 %all-to-all-start = ((bf16[64,16,3072]{2,1,0:T(8,128)(2,1)}), bf16[64,16,3072]{2,1,0:T(8,128)(2,1)}, u32[]{:S(2)}, u32[]{:S(2)}) async-start(bf16[64,16,3072]{2,1,0:T(8,128)(2,1)} %gather_fusion), calls=%async_computation | async-start | bytes 12582912 | tf_op jit(solution)/shard_map/all_to_all | solution.py:75
  122.4 0.2 all-reduce.4.cloned.1.call-start
  122.7 0.9 gather_fusion.6
  123.6 0.1 fusion.3
  123.6 0.1 reshape.70
  123.7 0.0 copy-done.4
  123.7 4.4 %convolution_convert_fusion.1 = bf16[1024,128]{1,0:T(8,128)(2,1)} fusion(bf16[1024,1536]{1,0:T(8,128)(2,1)} %bitcast.36, bf16[1536,128]{1,0:T(8,128)(2,1)S(1)} %copy-done.4), kind=kOutput, calls=%fused_computation.18 | convolution fusion | flops 402784256 | bytes 3801088 | tf_op jit(solution)/shard_map/dot_general | solution.py:22
  128.1 0.0 all-reduce.4.cloned.1.call-update
  128.1 79.1 %all-to-all-done = bf16[64,16,3072]{2,1,0:T(8,128)(2,1)} async-done(((bf16[64,16,3072]{2,1,0:T(8,128)(2,1)}), bf16[64,16,3072]{2,1,0:T(8,128)(2,1)}, u32[]{:S(2)}, u32[]{:S(2)}) %all-to-all-start) | async-done | bytes 6291488 | tf_op jit(solution)/shard_map/all_to_all | solution.py:75
  207.2 6.3 %gather_fusion.3 = bf16[64,16,3072]{2,1,0:T(8,128)(2,1)} fusion(bf16[64,16,3072]{2,1,0:T(8,128)(2,1)} %all-to-all-done, s32[1024]{0:T(1024)S(1)} %pad_clamp_fusion), kind=kCustom, calls=%fused_computation.3 | custom fusion | bytes 12583168 | tf_op jit(solution)/shard_map/gather | solution.py:86
  213.5 0.0 copy-start.2
  213.5 0.0 reduce-scatter.2.cloned.1.call-done
  213.5 6.8 %multiply_reduce_fusion = f32[1024]{0:T(1024)S(1)} fusion(bf16[1024,3072]{1,0:T(8,128)(2,1)} %reduce-scatter.2.cloned.1.call-done, bf16[64,16,3072]{2,1,0:T(8,128)(2,1)} %gather_fusion.3), kind=kLoop, calls=%fused_computation.14 | loop fusion | flops 15727616 | bytes 12587008 | tf_op jit(solution)/shard_map/reduce_sum | solution.py:31
  220.3 0.0 all-reduce.4.cloned.1.call-done
  220.3 0.0 copy-done.2
  220.3 0.0 copy-start.3
  220.3 8.9 %multiply_reduce_fusion.1 = (f32[1024]{0:T(1024)S(1)}, f32[1024,3072]{1,0:T(8,128)}) fusion(bf16[1024,128]{1,0:T(8,128)(2,1)} %all-reduce.4.cloned.1.call-done, bf16[128,3072]{1,0:T(8,128)(2,1)S(1)} %copy-done.2, bf16[1024,3072]{1,0:T(8,128)(2,1)} %reduce-scatter.2.cloned.1.call-done, bf16[1024,3072]{1,0:T(8,128)(2,1)} %bitcast.33), kind=kOutput, calls=%fused_computation.15 | convolution fusion | flops 824179712 | bytes 26218496 | tf_op jit(solution)/shard_map/dot_general | solution.py:25
  229.2 5.4 %all-reduce.1 = (f32[1024]{0:T(1024)S(1)}, f32[1024]{0:T(1024)S(1)}) all-reduce(f32[1024]{0:T(1024)S(1)} %get-tuple-element.8, f32[1024]{0:T(1024)S(1)} %multiply_reduce_fusion), channel_id=1, replica_groups=mesh['grp'=64,'tp'=2] {'tp'}, use_global_device_ids=true, to_apply=%region_5.6 | all-reduce | flops 2048 | bytes 16384 | tf_op jit(solution)/shard_map/psum | solution.py:28
  234.6 0.0 copy-done.3
  234.6 0.0 copy-start.1
  234.6 16.4 %fusion.1 = (bf16[1024,3072]{1,0:T(8,128)(2,1)}, bf16[1024,3072]{1,0:T(8,128)(2,1)}) fusion(bf16[1024,3072]{1,0:T(8,128)(2,1)} %reduce-scatter.2.cloned.1.call-done, bf16[64,16,3072]{2,1,0:T(8,128)(2,1)} %gather_fusion.3, f32[1024]{0:T(1024)S(1)} %get-tuple-element.10, f32[3072]{0:T(1024)S(1)} %copy-done.3, f32[1024]{0:T(1024)S(1)} %reshape.70, ...), kind=kLoop, calls=%fused_computation.12 | loop fusion | flops 31457280 | bytes 37773312 | tf_op jit(solution)/shard_map/convert_element_type | solution.py:43
  251.0 0.0 copy-done.1
  (10 shorter events, 0.1 us)
Async XLA Ops:
  7.2 16.2 %copy-start = (bf16[1024,1536]{1,0:T(8,128)(2,1)S(1)}, bf16[1024,1536]{1,0:T(8,128)(2,1)}, u32[]{:S(2)}) copy-start(bf16[1024,1536]{1,0:T(8,128)(2,1)} %param.9) | copy-start | bytes 9437188
  12.5 17.6 %all-to-all-start.1 = ((s32[64,1,2]{2,1,0:T(1,128)}), s32[64,1,2]{2,1,0:T(1,128)S(1)}, u32[]{:S(2)}, u32[]{:S(2)}) async-start(s32[64,1,2]{2,1,0:T(1,128)} %copy.11), calls=%async_computation.1 | async-start | bytes 65536 | tf_op jit(solution)/shard_map/all_to_all | solution.py:82
  30.1 44.7 %all-to-all-start.2 = ((bf16[64,16,1536]{2,1,0:T(8,128)(2,1)}), bf16[64,16,1536]{2,1,0:T(8,128)(2,1)}, u32[]{:S(2)}, u32[]{:S(2)}) async-start(bf16[64,16,1536]{2,1,0:T(8,128)(2,1)} %gather_fusion.4), calls=%async_computation.2 | async-start | bytes 6291456 | tf_op jit(solution)/shard_map/all_to_all | solution.py:68
  37.1 176.4 %reduce-scatter.2.cloned.1.call-start = ((), (), s32[]{:S(2)}) async-start(), calls=%async_computation.4 | async-start | bytes 18874368 | tf_op jit(solution)/shard_map/reduce_scatter | solution.py:19
  111.4 12.3 %copy-start.4 = (bf16[1536,128]{1,0:T(8,128)(2,1)S(1)}, bf16[1536,128]{1,0:T(8,128)(2,1)}, u32[]{:S(2)}) copy-start(bf16[1536,128]{1,0:T(8,128)(2,1)} %param.12) | copy-start | bytes 1179652
  111.4 95.8 %all-to-all-start = ((bf16[64,16,3072]{2,1,0:T(8,128)(2,1)}), bf16[64,16,3072]{2,1,0:T(8,128)(2,1)}, u32[]{:S(2)}, u32[]{:S(2)}) async-start(bf16[64,16,3072]{2,1,0:T(8,128)(2,1)} %gather_fusion), calls=%async_computation | async-start | bytes 12582912 | tf_op jit(solution)/shard_map/all_to_all | solution.py:75
  122.4 97.9 %all-reduce.4.cloned.1.call-start = ((), (), s32[]{:S(2)}) async-start(), calls=%async_computation.5 | async-start | bytes 524288 | tf_op jit(solution)/shard_map/psum | solution.py:23
  213.5 6.8 %copy-start.2 = (bf16[128,3072]{1,0:T(8,128)(2,1)S(1)}, bf16[128,3072]{1,0:T(8,128)(2,1)}, u32[]{:S(2)}) copy-start(bf16[128,3072]{1,0:T(8,128)(2,1)} %param.13) | copy-start | bytes 2359300
  220.3 14.3 %copy-start.3 = (f32[3072]{0:T(1024)S(1)}, f32[3072]{0:T(1024)}, u32[]{:S(2)}) copy-start(f32[3072]{0:T(1024)} %param.14) | copy-start | bytes 36868
  234.6 16.4 %copy-start.1 = (bf16[1024,1536]{1,0:T(8,128)(2,1)S(1)}, bf16[1024,1536]{1,0:T(8,128)(2,1)}, u32[]{:S(2)}) copy-start(bf16[1024,1536]{1,0:T(8,128)(2,1)} %param.9) | copy-start | bytes 9437188
Sparse Core Ops, SparseCore 0:
  105.0 27.0 reduce-scatter.1
  134.6 25.1 all-reduce.3
where the time goes:
time: 258 us
  waiting for transfers between devices  120 us (47%)
  matrix products  39 us (15%)
  starting transfers between devices  29.2 us (11%)
  local copies, waits for them, and re-layouts  25 us (10%)
  other arithmetic  24.1 us (9%)
  between operations  15 us (6%)
  blocking collectives  5.38 us (2%)
    all_to_all x1, waiting for transfers between devices, local(): lax.all_to_all(residual.reshape(group_total, block_size, residual_width)[...  79.1 us
    all_to_all x1, waiting for transfers between devices, local(): lax.all_to_all(context.reshape(group_total, block_size, context_width)[se...  36.8 us
    dot_general x1, matrix products, layer_rows(): jnp.dot(context_rows, out_weight, preferred_element_type=jnp.float32)  25.8 us
    convert_element_type x1, other arithmetic, layer_rows(): reference_rows = (reference_hidden * lax.rsqrt(square_sums[1] / full_widt...  16.4 us
    all_to_all x1, starting transfers between devices, local(): lax.all_to_all(residual.reshape(group_total, block_size, residual_width)[...  11.1 us
    all_to_all x1, starting transfers between devices, local(): lax.all_to_all(meta_sent, 'grp', split_axis=0, concat_axis=0, tiled=True)  10.8 us
    dot_general x1, matrix products, layer_rows(): jnp.dot(adapter_full, adapter_up, preferred_element_type=jnp.float32)  8.86 us
    all_to_all x1, starting transfers between devices, local(): lax.all_to_all(context.reshape(group_total, block_size, context_width)[se...  7.02 us
  transfers between devices with their start and end apart: 5, of which 3 were waited for; matrix products, arithmetic and copies ran while one was open for 11% of the time, Pallas kernels for 0%

commit v1 on v0

v1 whole, which is shorter than its diff:
```python
import functools

import jax
import jax.numpy as jnp
from jax import lax
from jax.experimental import pallas as pl
from jax.experimental.pallas import tpu as pltpu
from jax.sharding import PartitionSpec as P

EPSILON = 1e-05
MESH = pl.DeviceIdType.MESH

GROUPS = 64
SIDE = 4
BLK = 16
ROWS = 1024
KDIM = 1536
HALF = 3072
FULL = 6144
RANK = 128
PER = 16
MB = PER * BLK
NB = GROUPS // PER
CW = 512
NC = HALF // CW
MSG = HALF + RANK


def send_offsets():
    def distance(o):
        return sum(min(v, SIDE - v) for v in o)

    every = [(z, y, x) for z in range(SIDE) for y in range(SIDE) for x in range(SIDE)]
    every.remove((0, 0, 0))
    order = []
    for o in sorted(every, key=distance):
        for turn in (o, (o[1], o[2], o[0]), (o[2], o[0], o[1])):
            for w in (turn, tuple((SIDE - v) % SIDE for v in turn)):
                if w not in order:
                    order.append(w)
    order.append((0, 0, 0))
    return [(z * SIDE + y) * SIDE + x for z, y, x in order]


def packed_offsets():
    codes = send_offsets() + [0]
    return [sum(codes[5 * w + e] << (6 * e) for e in range(5)) for w in range(13)]


def target(j, me):
    word_at, lane = j // 5, j % 5
    word = jnp.int32(0)
    for index, value in enumerate(packed_offsets()):
        word = jnp.where(word_at == index, jnp.int32(value), word)
    code = (word >> (6 * lane)) & 63
    result = jnp.int32(0)
    for unit in (16, 4, 1):
        step = (code // unit) % SIDE
        result = result + ((me // unit) % SIDE + step) % SIDE * unit
    return result


def route_kernel(
    meta,
    ctx_hbm,
    res_hbm,
    w_hbm,
    down_hbm,
    up_hbm,
    gain_hbm,
    rows_out,
    aux_out,
    ctx_v,
    res_v,
    w_v,
    down_v,
    up_v,
    gain_v,
    lhs,
    own,
    hid,
    xs,
    xr,
    a_send,
    a_recv,
    a_full,
    s_send,
    s_recv,
    msg,
    aux,
    load_sem,
    w_sem,
    xs_sem,
    xr_sem,
    as_sem,
    ar_sem,
    ss_sem,
    sr_sem,
    ms_sem,
    mr_sem,
    us_sem,
    ur_sem,
):
    me = lax.axis_index("grp")
    tp = lax.axis_index("tp")
    mate = 1 - tp

    barrier = pltpu.get_barrier_semaphore()

    def greet(i, carry):
        pl.semaphore_signal(
            barrier, inc=1, device_id=((me + i) % GROUPS, tp), device_id_type=MESH
        )
        return carry

    loads = [
        pltpu.make_async_copy(ctx_hbm, ctx_v, load_sem.at[0]),
        pltpu.make_async_copy(down_hbm, down_v, load_sem.at[1]),
        pltpu.make_async_copy(res_hbm, res_v, load_sem.at[2]),
        pltpu.make_async_copy(up_hbm, up_v, load_sem.at[3]),
        pltpu.make_async_copy(gain_hbm, gain_v, load_sem.at[4]),
    ]

    def weight_load(c):
        half = jnp.where(c < NC, mate, tp)
        start = pl.multiple_of(half * HALF + (c % NC) * CW, CW)
        return pltpu.make_async_copy(w_hbm.at[:, pl.ds(start, CW)], w_v.at[c], w_sem.at[c])

    def mate_copy(src, dst, ssem, rsem):
        return pltpu.make_async_remote_copy(
            src_ref=src,
            dst_ref=dst,
            send_sem=ssem,
            recv_sem=rsem,
            device_id=(me, mate),
            device_id_type=MESH,
        )

    def half_copy(k, c):
        return mate_copy(xs.at[k, c], xr.at[k, c], xs_sem.at[k, c], xr_sem.at[k, c])

    def adapter_copy(k):
        return mate_copy(a_send.at[k], a_recv.at[k], as_sem.at[k], ar_sem.at[k])

    def square_copy(k):
        return mate_copy(s_send.at[k], s_recv.at[k], ss_sem.at[k], sr_sem.at[k])

    def row_copy(j, there, slot):
        return pltpu.make_async_remote_copy(
            src_ref=msg.at[j],
            dst_ref=rows_out.at[slot],
            send_sem=ms_sem.at[j],
            recv_sem=mr_sem.at[slot],
            device_id=(there, tp),
            device_id_type=MESH,
        )

    def aux_copy(j, there, slot):
        return pltpu.make_async_remote_copy(
            src_ref=aux.at[j],
            dst_ref=aux_out.at[slot],
            send_sem=us_sem.at[j],
            recv_sem=ur_sem.at[slot],
            device_id=(there, tp),
            device_id_type=MESH,
        )

    loads[0].start()
    loads[1].start()

    def start_weight(c, carry):
        weight_load(c).start()
        return carry

    lax.fori_loop(0, 2 * NC, start_weight, 0)
    for copy in loads[2:]:
        copy.start()

    lax.fori_loop(1, GROUPS, greet, 0)
    pl.semaphore_signal(barrier, inc=1, device_id=(me, mate), device_id_type=MESH)
    loads[0].wait()
    loads[1].wait()
    pl.semaphore_wait(barrier, GROUPS)

    lane = lax.broadcasted_iota(jnp.int32, (BLK, RANK), 1)
    token = lax.broadcasted_iota(jnp.int32, (BLK, RANK), 0)
    live_count = meta[2 * GROUPS]

    def batch(k, carry):
        def gather(i, c):
            there = target(k * PER + i, me)
            lhs[i] = ctx_v[meta[there]]
            return c

        lax.fori_loop(0, PER, gather, 0)
        a_send[k] = jnp.dot(
            lhs[...].reshape(MB, KDIM), down_v[...], preferred_element_type=jnp.float32
        )
        adapter_copy(k).start()

        def away(c, carry2):
            @pl.when(k == 0)
            def _():
                weight_load(c).wait()

            xs[k, c] = jnp.dot(
                lhs[...].reshape(MB, KDIM), w_v[c], preferred_element_type=jnp.float32
            ).astype(jnp.bfloat16)
            half_copy(k, c).start()
            return carry2

        lax.fori_loop(0, NC, away, 0)

        def home(c, carry2):
            @pl.when(k == 0)
            def _():
                weight_load(NC + c).wait()

            own[c] = jnp.dot(
                lhs[...].reshape(MB, KDIM), w_v[NC + c], preferred_element_type=jnp.float32
            ).astype(jnp.bfloat16)
            return carry2

        lax.fori_loop(0, NC, home, 0)

        @pl.when(k == 0)
        def _():
            for copy in loads[2:]:
                copy.wait()

        adapter_copy(k).wait_recv()
        a_full[...] = (a_send[k] + a_recv[k]).astype(jnp.bfloat16)

        def lift(c, carry2):
            cols = pl.ds(pl.multiple_of(c * CW, CW), CW)
            hid[c] = jnp.dot(a_full[...], up_v[:, cols], preferred_element_type=jnp.float32)
            return carry2

        lax.fori_loop(0, NC, lift, 0)

        def arrive(c, carry2):
            half_copy(k, c).wait_recv()
            return carry2

        lax.fori_loop(0, NC, arrive, 0)

        def squares(i, carry2):
            block = meta[target(k * PER + i, me)]
            at = pl.ds(pl.multiple_of(i * BLK, BLK), BLK)
            ref_sum = jnp.zeros((BLK, CW), jnp.float32)
            pol_sum = jnp.zeros((BLK, CW), jnp.float32)
            for c in range(NC):
                h = (
                    own[c, at, :].astype(jnp.float32)
                    + xr[k, c, at, :].astype(jnp.float32)
                    + res_v[block, :, c * CW : (c + 1) * CW].astype(jnp.float32)
                )
                q = h + hid[c, at, :]
                hid[c, at, :] = h
                ref_sum = ref_sum + h * h
                pol_sum = pol_sum + q * q
            s_send[k, at, :] = jnp.where(
                lane < RANK // 2,
                jnp.sum(ref_sum, axis=1, keepdims=True),
                jnp.sum(pol_sum, axis=1, keepdims=True),
            )
            return carry2

        lax.fori_loop(0, PER, squares, 0)
        square_copy(k).start()
        square_copy(k).wait_recv()

        def finish(i, carry2):
            j = k * PER + i
            there = target(j, me)
            block = meta[there]
            at = pl.ds(pl.multiple_of(i * BLK, BLK), BLK)
            total = s_send[k, at, :] + s_recv[k, at, :]
            live = jnp.where(block * BLK + token < live_count, 1.0, 0.0)
            scale = lax.rsqrt(total / FULL + EPSILON) * live
            ref_scale = scale[:, 0:1]
            pol_scale = scale[:, RANK // 2 : RANK // 2 + 1]
            unmasked = lax.rsqrt(total / FULL + EPSILON)
            ratio = pol_scale / unmasked[:, 0:1]
            for c in range(NC):
                cols = slice(c * CW, (c + 1) * CW)
                msg[j, :, cols] = (hid[c, at, :] * ref_scale * gain_v[:, cols]).astype(
                    jnp.bfloat16
                )
            msg[j, :, HALF:] = a_full[at, :]
            line = jnp.where(
                lane == token, ratio, jnp.where(lane == token + BLK, pol_scale, 0.0)
            )
            seat = jnp.where(
                (token == 0) & (lane == 2 * BLK),
                meta[GROUPS + there].astype(jnp.float32),
                0.0,
            )
            aux[j] = jnp.sum(line + seat, axis=0, keepdims=True)

            @pl.when(j < GROUPS - 1)
            def _():
                row_copy(j, there, me).start()
                aux_copy(j, there, me).start()

            return carry2

        lax.fori_loop(0, PER, finish, 0)
        return carry

    lax.fori_loop(0, NB, batch, 0)

    keep_rows = pltpu.make_async_copy(msg.at[GROUPS - 1], rows_out.at[me], load_sem.at[0])
    keep_aux = pltpu.make_async_copy(aux.at[GROUPS - 1], aux_out.at[me], load_sem.at[1])
    keep_rows.start()
    keep_aux.start()

    def drain_mate(k, carry):
        adapter_copy(k).wait_send()
        square_copy(k).wait_send()

        def drain_half(c, carry2):
            half_copy(k, c).wait_send()
            return carry2

        lax.fori_loop(0, NC, drain_half, 0)
        return carry

    lax.fori_loop(0, NB, drain_mate, 0)
    keep_rows.wait()
    keep_aux.wait()

    def drain(i, carry):
        source = (me + i) % GROUPS
        aux_copy(i - 1, source, source).wait()
        row_copy(i - 1, source, source).wait()
        return carry

    lax.fori_loop(1, GROUPS, drain, 0)


def route(meta, context, residual, out_weight, adapter_down, adapter_up, gain):
    any_space = pl.BlockSpec(memory_space=pl.ANY)
    dma = pltpu.SemaphoreType.DMA
    bf16, f32 = jnp.bfloat16, jnp.float32
    return pl.pallas_call(
        route_kernel,
        out_shape=(
            jax.ShapeDtypeStruct((GROUPS, BLK, MSG), bf16),
            jax.ShapeDtypeStruct((GROUPS, 1, RANK), f32),
        ),
        in_specs=[pl.BlockSpec(memory_space=pltpu.SMEM)] + [any_space] * 6,
        out_specs=(any_space, any_space),
        scratch_shapes=[
            pltpu.VMEM((GROUPS, BLK, KDIM), bf16),
            pltpu.VMEM((GROUPS, BLK, HALF), bf16),
            pltpu.VMEM((2 * NC, KDIM, CW), bf16),
            pltpu.VMEM((KDIM, RANK), bf16),
            pltpu.VMEM((RANK, HALF), bf16),
            pltpu.VMEM((1, HALF), f32),
            pltpu.VMEM((PER, BLK, KDIM), bf16),
            pltpu.VMEM((NC, MB, CW), bf16),
            pltpu.VMEM((NC, MB, CW), f32),
            pltpu.VMEM((NB, NC, MB, CW), bf16),
            pltpu.VMEM((NB, NC, MB, CW), bf16),
            pltpu.VMEM((NB, MB, RANK), f32),
            pltpu.VMEM((NB, MB, RANK), f32),
            pltpu.VMEM((MB, RANK), bf16),
            pltpu.VMEM((NB, MB, RANK), f32),
            pltpu.VMEM((NB, MB, RANK), f32),
            pltpu.VMEM((GROUPS, BLK, MSG), bf16),
            pltpu.VMEM((GROUPS, 1, RANK), f32),
            dma((5,)),
            dma((2 * NC,)),
            dma((NB, NC)),
            dma((NB, NC)),
            dma((NB,)),
            dma((NB,)),
            dma((NB,)),
            dma((NB,)),
            dma((GROUPS,)),
            dma((GROUPS,)),
            dma((GROUPS,)),
            dma((GROUPS,)),
        ],
        compiler_params=pltpu.CompilerParams(
            collective_id=0, has_side_effects=True, vmem_limit_bytes=60 * 2**20
        ),
        cost_estimate=pl.CostEstimate(
            flops=2 * ROWS * KDIM * FULL, bytes_accessed=48 * 2**20, transcendentals=0
        ),
        name="route",
    )(meta, context, residual, out_weight, adapter_down, adapter_up, gain)


OUT_PER = 8


def place_kernel(sources, *refs):
    rows = refs[:OUT_PER]
    lines = refs[OUT_PER : 2 * OUT_PER]
    up, gain, policy, reference, inner = refs[2 * OUT_PER :]
    for e in range(OUT_PER):
        inner[e * BLK : (e + 1) * BLK, :] = rows[e][0, :, HALF:]
    lane = lax.broadcasted_iota(jnp.int32, (BLK, RANK), 1)
    token = lax.broadcasted_iota(jnp.int32, (BLK, RANK), 0)
    scales = []
    for e in range(OUT_PER):
        line = jnp.broadcast_to(lines[e][0], (BLK, RANK))
        scales.append(
            (
                jnp.sum(jnp.where(lane == token, line, 0.0), axis=1, keepdims=True),
                jnp.sum(jnp.where(lane == token + BLK, line, 0.0), axis=1, keepdims=True),
            )
        )
    for c in range(NC):
        cols = slice(c * CW, (c + 1) * CW)
        delta = jnp.dot(inner[...], up[:, cols], preferred_element_type=jnp.float32)
        for e in range(OUT_PER):
            at = slice(e * BLK, (e + 1) * BLK)
            ratio, pol_scale = scales[e]
            ref_rows = rows[e][0, :, cols]
            reference[at, cols] = ref_rows
            policy[at, cols] = (
                ref_rows.astype(jnp.float32) * ratio
                + delta[at, :] * pol_scale * gain[:, cols]
            ).astype(jnp.bfloat16)


def place(sources, rows, lines, adapter_up, gain):
    def block_at(e):
        return lambda i, table: (table[i * OUT_PER + e], 0, 0)

    whole = lambda i, table: (0, 0)
    out_spec = pl.BlockSpec((OUT_PER * BLK, HALF), lambda i, table: (i, 0))
    return pl.pallas_call(
        place_kernel,
        grid_spec=pltpu.PrefetchScalarGridSpec(
            num_scalar_prefetch=1,
            grid=(GROUPS // OUT_PER,),
            in_specs=[pl.BlockSpec((1, BLK, MSG), block_at(e)) for e in range(OUT_PER)]
            + [pl.BlockSpec((1, 1, RANK), block_at(e)) for e in range(OUT_PER)]
            + [pl.BlockSpec((RANK, HALF), whole), pl.BlockSpec((1, HALF), whole)],
            out_specs=[out_spec, out_spec],
            scratch_shapes=[pltpu.VMEM((OUT_PER * BLK, RANK), jnp.bfloat16)],
        ),
        out_shape=[jax.ShapeDtypeStruct((ROWS, HALF), jnp.bfloat16)] * 2,
        compiler_params=pltpu.CompilerParams(vmem_limit_bytes=48 * 2**20),
        name="place",
    )(sources, *([rows] * OUT_PER), *([lines] * OUT_PER), adapter_up, gain)


def local(
    context,
    residual,
    out_weight,
    adapter_down,
    adapter_up,
    norm_gain,
    lengths,
    route_group,
    route_slot,
):
    position = jnp.arange(GROUPS, dtype=jnp.int32)
    chosen = route_group[0][None, :] == position[:, None]
    block_for = jnp.sum(jnp.where(chosen, position[None, :], 0), axis=1)
    seat_for = jnp.sum(jnp.where(chosen, route_slot[0][None, :], 0), axis=1)
    meta = jnp.concatenate([block_for, seat_for, lengths]).astype(jnp.int32)
    gain = norm_gain[None, :]
    rows, lines = route(
        meta,
        context.reshape(GROUPS, BLK, KDIM),
        residual.reshape(GROUPS, BLK, HALF),
        out_weight,
        adapter_down,
        adapter_up,
        gain,
    )
    seats = lines[:, 0, 2 * BLK].astype(jnp.int32)
    sources = jnp.sum(
        jnp.where(seats[None, :] == position[:, None], position[None, :], 0), axis=1
    ).astype(jnp.int32)
    return tuple(place(sources, rows, lines, adapter_up, gain))


def solution(mesh):
    in_specs = (
        P("grp", "tp"),
        P("grp", "tp"),
        P("tp", None),
        P("tp", None),
        P(None, "tp"),
        P("tp"),
        P("grp"),
        P("grp", None),
        P("grp", None),
    )
    out_specs = (P("grp", "tp"), P("grp", "tp"))
    return jax.shard_map(local, mesh=mesh, in_specs=in_specs, out_specs=out_specs, check_vma=False)
```

time: 258 us -> 148 us (0.57)
  the two profiles are of different devices: /device:TPU:11 before, /device:TPU:1 now
where the time goes in v1:
time: 148 us; the launch traced here: 147 us
  Pallas kernels  142 us (96%)
  other arithmetic  3.61 us (2%)
    pallas_call x1, Pallas kernels, route(): pl.pallas_call(route_kernel, out_shape=(jax.ShapeDtypeStruct((GROUPS, BLK...  130 us
    pallas_call x1, Pallas kernels, place(): pl.pallas_call(place_kernel, grid_spec=pltpu.PrefetchScalarGridSpec(num_s...  11.8 us

profile of v1, /device:TPU:1, one launch (start us, length us, event | category | flops | bytes accessed | tf_op | source)
XLA Modules:
  0.0 147.3 jit_solution(3331520993946029750)
XLA Ops:
  1.3 0.8 select_reduce_fusion.2
  2.1 0.6 pad_add_fusion.meta
  2.7 0.0 copy-start.1
  2.7 0.0 copy-start.2
  2.7 129.9 %route.1 = (bf16[64,16,3200]{2,1,0:T(8,128)(2,1)}, f32[64,1,128]{2,1,0:T(1,128)}) custom-call(s32[129]{0:T(256)} %pad_add_fusion.meta, bf16[64,16,1536]{2,1,0:T(8,128)(2,1)} %bitcast.10, bf16[64,16,3072]{2,1,0:T(8,128)(2,1)} %bitcast.9, bf16[1536,6144]{1,0:T(8,128)(2,1)} %w_hbm.1, bf16[1536,128]{1,0:T(8,128)(2,1)} %down_hbm.1, bf16[128,3072]{1,0:T(8,128)(2,1)} %refs_16_.1, ...), custom_call_target="tpu_custom_call" | custom-call | flops 19327352832 | bytes 50331648 | tf_op jit(solution)/shard_map/route/pallas_call | solution.py:346
  132.6 2.1 %convert_reduce_fusion = s32[64]{0:T(128)S(1)} fusion(f32[64,1,128]{2,1,0:T(1,128)} %get-tuple-element.4.refs_8_.refs_9_.refs_10_.refs_11_.refs_12_.refs_13_.refs_14_.refs_15_), kind=kLoop, calls=%fused_computation.2 | loop fusion | flops 64 | bytes 512 | tf_op jit(solution)/shard_map/convert_element_type | solution.py:479
  134.7 0.1 select_reduce_fusion.sources
  134.8 0.0 copy-done.1
  134.8 0.0 copy-done.2
  134.8 0.0 copy-start
  134.8 0.7 copy-done
  135.6 11.8 %place.1 = (bf16[1024,3072]{1,0:T(8,128)(2,1)}, bf16[1024,3072]{1,0:T(8,128)(2,1)}) custom-call(s32[64]{0:T(128)S(1)} %select_reduce_fusion.sources, bf16[64,16,3200]{2,1,0:T(8,128)(2,1)} %get-tuple-element.5.refs_0_.refs_1_.refs_2_.refs_3_.refs_4_.refs_5_.refs_6_.refs_7_, ...), custom_call_target="tpu_custom_call" | custom-call | tf_op jit(solution)/shard_map/place/pallas_call | solution.py:436
Async XLA Ops:
  2.7 132.1 %copy-start.1 = (bf16[128,3072]{1,0:T(8,128)(2,1)S(1)}, bf16[128,3072]{1,0:T(8,128)(2,1)}, u32[]{:S(2)}) copy-start(bf16[128,3072]{1,0:T(8,128)(2,1)} %refs_16_.1) | copy-start | bytes 2359300
  2.7 132.1 %copy-start.2 = (f32[3072]{0:T(1024)S(1)}, f32[3072]{0:T(1024)}, u32[]{:S(2)}) copy-start(f32[3072]{0:T(1024)} %param.14) | copy-start | bytes 36868
  134.8 0.8 copy-start

commit v2 on v0

v2 whole, which is shorter than its diff:
```python
import functools

import jax
import jax.numpy as jnp
from jax import lax
from jax.experimental import pallas as pl
from jax.experimental.pallas import tpu as pltpu
from jax.sharding import PartitionSpec as P

EPSILON = 1e-05
MESH = pl.DeviceIdType.MESH

GROUPS = 64
SIDE = 4
BLK = 16
ROWS = 1024
KDIM = 1536
HALF = 3072
FULL = 6144
RANK = 128
PER = 16
MB = PER * BLK
NR = GROUPS // PER
CW = 512
NC = HALF // CW
UNITS = NC * NR
RING = 4
WRING = 4


def send_offsets():
    def distance(o):
        return sum(min(v, SIDE - v) for v in o)

    def negative(o):
        return tuple((SIDE - v) % SIDE for v in o)

    every = [(z, y, x) for z in range(SIDE) for y in range(SIDE) for x in range(SIDE)]
    every.sort(key=distance)
    alone = [o for o in every if o == negative(o) and o != (0, 0, 0)] + [(0, 0, 0)]
    pairs = list(zip(alone[::2], alone[1::2]))
    seen = set(alone)
    for o in every:
        if o in seen:
            continue
        for turn in (o, (o[1], o[2], o[0]), (o[2], o[0], o[1])):
            if turn not in seen:
                pairs.append((turn, negative(turn)))
                seen.update(pairs[-1])
    pairs.sort(key=lambda p: 99 if (0, 0, 0) in p else distance(p[0]) + distance(p[1]))
    return [(z * SIDE + y) * SIDE + x for pair in pairs for z, y, x in pair]


def packed_offsets():
    codes = send_offsets() + [0]
    return [sum(codes[5 * w + e] << (6 * e) for e in range(5)) for w in range(13)]


def target(j, me):
    word_at = (j * 13) >> 6
    word = jnp.int32(0)
    for index, value in enumerate(packed_offsets()):
        word = jnp.where(word_at == index, jnp.int32(value), word)
    code = word >> (6 * (j - 5 * word_at))
    return (
        ((me & 48) + (code & 48)) & 48
        | ((me & 12) + (code & 12)) & 12
        | ((me & 3) + (code & 3)) & 3
    )


def route_kernel(
    meta,
    length,
    ctx_hbm,
    res_hbm,
    w_hbm,
    down_hbm,
    up_hbm,
    rows_out,
    inner_out,
    lines_out,
    table_out,
    up_v,
    ctx_v,
    res_v,
    w_v,
    down_v,
    lhs,
    own,
    xs,
    xr,
    delta,
    ref_sq,
    pol_sq,
    a_send,
    a_recv,
    a_full,
    s_send,
    s_recv,
    msg,
    line,
    load_sem,
    w_sem,
    xs_sem,
    xr_sem,
    as_sem,
    ar_sem,
    ss_sem,
    sr_sem,
    ms_sem,
    mr_sem,
    small_sem,
):
    me = lax.axis_index("grp")
    tp = lax.axis_index("tp")
    mate = 1 - tp

    barrier = pltpu.get_barrier_semaphore()

    def greet(i, carry):
        pl.semaphore_signal(
            barrier, inc=1, device_id=((me + i) % GROUPS, tp), device_id_type=MESH
        )
        return carry

    loads = [
        pltpu.make_async_copy(ctx_hbm, ctx_v, load_sem.at[0]),
        pltpu.make_async_copy(down_hbm, down_v, load_sem.at[1]),
        pltpu.make_async_copy(up_hbm, up_v, load_sem.at[2]),
        pltpu.make_async_copy(res_hbm, res_v, load_sem.at[3]),
    ]

    def weight_load(c, away):
        half = mate if away else tp
        start = pl.multiple_of(half * HALF + c * CW, CW)
        slot = 2 * (c % WRING) + (0 if away else 1)
        return pltpu.make_async_copy(
            w_hbm.at[:, pl.ds(start, CW)], w_v.at[slot], w_sem.at[slot]
        )

    def mate_copy(src, dst, ssem, rsem):
        return pltpu.make_async_remote_copy(
            src_ref=src,
            dst_ref=dst,
            send_sem=ssem,
            recv_sem=rsem,
            device_id=(me, mate),
            device_id_type=MESH,
        )

    def half_copy(u):
        return mate_copy(xs.at[u % RING], xr.at[u], xs_sem.at[u], xr_sem.at[u])

    def adapter_copy(r):
        return mate_copy(a_send.at[r], a_recv.at[r], as_sem.at[r], ar_sem.at[r])

    def square_copy(r):
        return mate_copy(s_send.at[r], s_recv.at[r], ss_sem.at[r], sr_sem.at[r])

    def far_copy(src, dst, ssem, rsem, there):
        return pltpu.make_async_remote_copy(
            src_ref=src,
            dst_ref=dst,
            send_sem=ssem,
            recv_sem=rsem,
            device_id=(there, tp),
            device_id_type=MESH,
        )

    def start_rows(c, j, there):
        far_copy(
            msg.at[c, j], rows_out.at[c, me], ms_sem.at[c], mr_sem.at[c], there
        ).start()

    def inner_copy(j, there, slot):
        return far_copy(
            a_full.at[j], inner_out.at[slot], small_sem.at[0], small_sem.at[1], there
        )

    def line_copy(j, there, slot):
        return far_copy(line.at[j], lines_out.at[slot], small_sem.at[2], small_sem.at[3], there)

    loads[0].start()
    loads[1].start()
    weight_load(0, True).start()
    weight_load(0, False).start()
    loads[2].start()
    loads[3].start()
    for c in range(1, WRING):
        weight_load(c, True).start()
        weight_load(c, False).start()

    lax.fori_loop(1, GROUPS, greet, 0)
    pl.semaphore_signal(barrier, inc=1, device_id=(me, mate), device_id_type=MESH)

    ref_sq[...] = jnp.zeros_like(ref_sq)
    pol_sq[...] = jnp.zeros_like(pol_sq)
    loads[0].wait()

    def gather(j, carry):
        lhs[j] = ctx_v[meta[0, j]]
        return carry

    lax.fori_loop(0, GROUPS, gather, 0)
    loads[1].wait()

    def squeeze(r, carry):
        at = pl.ds(pl.multiple_of(r * PER, PER), PER)
        a_send[r] = jnp.dot(
            lhs[at].reshape(MB, KDIM), down_v[...], preferred_element_type=jnp.float32
        )
        return carry

    lax.fori_loop(0, NR, squeeze, 0)
    pl.semaphore_wait(barrier, GROUPS)

    def start_adapter(r, carry):
        adapter_copy(r).start()
        return carry

    lax.fori_loop(0, NR, start_adapter, 0)

    lane = lax.broadcasted_iota(jnp.int32, (BLK, RANK), 1)
    token = lax.broadcasted_iota(jnp.int32, (BLK, RANK), 0)

    def unit(u, carry):
        @pl.when(u < UNITS)
        def _():
            c = u // NR
            r = u % NR
            at = pl.ds(pl.multiple_of(r * PER, PER), PER)

            @pl.when(r == 0)
            def _():
                weight_load(c, True).wait()

            @pl.when(u >= RING)
            def _():
                half_copy(u - RING).wait_send()

            xs[u % RING] = jnp.dot(
                lhs[at].reshape(MB, KDIM), w_v[2 * (c % WRING)], preferred_element_type=jnp.float32
            ).astype(jnp.bfloat16)
            half_copy(u).start()

            @pl.when(r == 0)
            def _():
                weight_load(c, False).wait()

            own[u % 2] = jnp.dot(
                lhs[at].reshape(MB, KDIM), w_v[2 * (c % WRING) + 1], preferred_element_type=jnp.float32
            ).astype(jnp.bfloat16)

            @pl.when((r == NR - 1) & (c + WRING < NC))
            def _():
                weight_load(c + WRING, True).start()
                weight_load(c + WRING, False).start()

        @pl.when(u == 1)
        def _():
            def adapt(r, c2):
                adapter_copy(r).wait_recv()
                at = pl.ds(pl.multiple_of(r * PER, PER), PER)
                a_full[at] = (
                    (a_send[r] + a_recv[r]).astype(jnp.bfloat16).reshape(PER, BLK, RANK)
                )
                return c2

            lax.fori_loop(0, NR, adapt, 0)
            loads[2].wait()
            loads[3].wait()

        @pl.when(u >= 1)
        def _():
            v = u - 1
            c = v // NR
            r = v % NR
            at = pl.ds(pl.multiple_of(r * PER, PER), PER)
            cols = pl.ds(pl.multiple_of(c * CW, CW), CW)
            delta[...] = jnp.dot(
                a_full[at].reshape(MB, RANK), up_v[:, cols], preferred_element_type=jnp.float32
            )
            half_copy(v).wait_recv()

            def finish(i0, c2):
                i = i0 + tp * (1 - 2 * (i0 % 2))
                j = r * PER + i
                block = meta[0, j]
                here = pl.ds(pl.multiple_of(i * BLK, BLK), BLK)
                h = (
                    own[v % 2, here, :].astype(jnp.float32)
                    + xr[v, here, :].astype(jnp.float32)
                    + res_v[block, :, cols].astype(jnp.float32)
                )
                msg[c, j] = h.astype(jnp.bfloat16)

                @pl.when(j < GROUPS - 1)
                def _():
                    start_rows(c, j, target(j, me))

                q = h + delta[here, :]
                h2 = h * h
                q2 = q * q
                ref_sum = ref_sq[j]
                pol_sum = pol_sq[j]
                for e in range(CW // RANK):
                    ref_sum = ref_sum + h2[:, e * RANK : (e + 1) * RANK]
                    pol_sum = pol_sum + q2[:, e * RANK : (e + 1) * RANK]
                ref_sq[j] = ref_sum
                pol_sq[j] = pol_sum
                return c2

            lax.fori_loop(0, PER, finish, 0)

        return carry

    lax.fori_loop(0, UNITS + 1, unit, 0)

    wide = lax.broadcasted_iota(jnp.int32, (MB, RANK), 1)

    def start_squares(r, carry):
        at = pl.ds(pl.multiple_of(r * PER, PER), PER)
        s_send[r] = jnp.where(
            wide < RANK // 2,
            jnp.sum(ref_sq[at].reshape(MB, RANK), axis=1, keepdims=True),
            jnp.sum(pol_sq[at].reshape(MB, RANK), axis=1, keepdims=True),
        )
        square_copy(r).start()
        return carry

    lax.fori_loop(0, NR, start_squares, 0)

    def factors(r, carry):
        square_copy(r).wait_recv()

        def one(i, c2):
            j = r * PER + i
            block = meta[0, j]
            here = pl.ds(pl.multiple_of(i * BLK, BLK), BLK)
            total = s_send[r, here, :] + s_recv[r, here, :]
            live = jnp.where(block * BLK + token < length[0], 1.0, 0.0)
            scale = lax.rsqrt(total / FULL + EPSILON) * live
            row = jnp.where(
                lane == token,
                scale[:, 0:1],
                jnp.where(lane == token + BLK, scale[:, RANK // 2 : RANK // 2 + 1], 0.0),
            )
            seat = jnp.where(
                (token == 0) & (lane == 2 * BLK), meta[1, j].astype(jnp.float32), 0.0
            )
            line[j] = jnp.sum(row + seat, axis=0, keepdims=True)

            @pl.when(j < GROUPS - 1)
            def _():
                there = target(j, me)
                inner_copy(j, there, me).start()
                line_copy(j, there, me).start()

            return c2

        lax.fori_loop(0, PER, one, 0)
        return carry

    lax.fori_loop(0, NR, factors, 0)

    last = GROUPS - 1
    keep = [
        pltpu.make_async_copy(msg.at[c, last], rows_out.at[c, me], w_sem.at[c])
        for c in range(NC)
    ]
    keep.append(pltpu.make_async_copy(a_full.at[last], inner_out.at[me], load_sem.at[0]))
    keep.append(pltpu.make_async_copy(line.at[last], lines_out.at[me], load_sem.at[1]))
    for copy in keep:
        copy.start()

    def drain_mate(r, carry):
        adapter_copy(r).wait_send()
        square_copy(r).wait_send()
        return carry

    lax.fori_loop(0, NR, drain_mate, 0)

    def drain_half(u, carry):
        half_copy(u).wait_send()
        return carry

    lax.fori_loop(UNITS - RING, UNITS, drain_half, 0)
    for copy in keep:
        copy.wait()

    others = pl.ds(0, last)
    for at, ref in enumerate((a_full, inner_out, line, lines_out)):
        pltpu.make_async_copy(ref.at[others], ref.at[others], small_sem.at[at]).wait()
    sheet = lines_out[...].reshape(GROUPS, RANK)
    seats = sheet[:, 2 * BLK : 2 * BLK + 1].astype(jnp.int32)
    source = lax.broadcasted_iota(jnp.int32, (GROUPS, RANK), 0)
    place_at = lax.broadcasted_iota(jnp.int32, (GROUPS, RANK), 1)
    table_out[...] = jnp.sum(
        jnp.where(seats == place_at, source, 0), axis=0, keepdims=True
    )
    for c in range(NC):
        sent = msg.at[c, others]
        came = rows_out.at[c, others]
        pltpu.make_async_copy(sent, sent, ms_sem.at[c]).wait()
        pltpu.make_async_copy(came, came, mr_sem.at[c]).wait()


def route(meta, length, context, residual, out_weight, adapter_down, adapter_up):
    any_space = pl.BlockSpec(memory_space=pl.ANY)
    scalars = pl.BlockSpec(memory_space=pltpu.SMEM)
    vector = pl.BlockSpec(memory_space=pltpu.VMEM)
    dma = pltpu.SemaphoreType.DMA
    bf16, f32 = jnp.bfloat16, jnp.float32
    return pl.pallas_call(
        route_kernel,
        out_shape=(
            jax.ShapeDtypeStruct((NC, GROUPS, BLK, CW), bf16),
            jax.ShapeDtypeStruct((GROUPS, BLK, RANK), bf16),
            jax.ShapeDtypeStruct((GROUPS, 1, RANK), f32),
            jax.ShapeDtypeStruct((1, RANK), jnp.int32),
            jax.ShapeDtypeStruct((RANK, HALF), bf16),
        ),
        in_specs=[scalars] * 2 + [any_space] * 5,
        out_specs=(any_space, any_space, vector, vector, vector),
        scratch_shapes=[
            pltpu.VMEM((GROUPS, BLK, KDIM), bf16),
            pltpu.VMEM((GROUPS, BLK, HALF), bf16),
            pltpu.VMEM((2 * WRING, KDIM, CW), bf16),
            pltpu.VMEM((KDIM, RANK), bf16),
            pltpu.VMEM((GROUPS, BLK, KDIM), bf16),
            pltpu.VMEM((2, MB, CW), bf16),
            pltpu.VMEM((RING, MB, CW), bf16),
            pltpu.VMEM((UNITS, MB, CW), bf16),
            pltpu.VMEM((MB, CW), f32),
            pltpu.VMEM((GROUPS, BLK, RANK), f32),
            pltpu.VMEM((GROUPS, BLK, RANK), f32),
            pltpu.VMEM((NR, MB, RANK), f32),
            pltpu.VMEM((NR, MB, RANK), f32),
            pltpu.VMEM((GROUPS, BLK, RANK), bf16),
            pltpu.VMEM((NR, MB, RANK), f32),
            pltpu.VMEM((NR, MB, RANK), f32),
            pltpu.VMEM((NC, GROUPS, BLK, CW), bf16),
            pltpu.VMEM((GROUPS, 1, RANK), f32),
            dma((4,)),
            dma((2 * WRING,)),
            dma((UNITS,)),
            dma((UNITS,)),
            dma((NR,)),
            dma((NR,)),
            dma((NR,)),
            dma((NR,)),
            dma((NC,)),
            dma((NC,)),
            dma((4,)),
        ],
        compiler_params=pltpu.CompilerParams(
            collective_id=0, has_side_effects=True, vmem_limit_bytes=VMEM_LIMIT
        ),
        cost_estimate=pl.CostEstimate(
            flops=2 * ROWS * KDIM * FULL, bytes_accessed=48 * 2**20, transcendentals=0
        ),
        name="route",
    )(
        meta,
        length,
        *[
            pltpu.with_memory_space_constraint(x, pltpu.HBM)
            for x in (context, residual, out_weight, adapter_down, adapter_up)
        ],
    )


VMEM_LIMIT = 44 * 2**20
PLACE_LIMIT = 24 * 2**20
OUT_PER = 8


def place_kernel(table, *refs):
    rows, inner, lines, up, gain, policy, reference, packed = refs
    step = pl.program_id(0)
    lane = lax.broadcasted_iota(jnp.int32, (BLK, RANK), 1)
    token = lax.broadcasted_iota(jnp.int32, (BLK, RANK), 0)
    sources = []
    scales = []
    for e in range(OUT_PER):
        source = table[step * OUT_PER + e]
        packed[e * BLK : (e + 1) * BLK, :] = inner[source]
        row = jnp.broadcast_to(lines[source], (BLK, RANK))
        sources.append(source)
        scales.append(
            (
                jnp.sum(jnp.where(lane == token, row, 0.0), axis=1, keepdims=True),
                jnp.sum(jnp.where(lane == token + BLK, row, 0.0), axis=1, keepdims=True),
            )
        )
    for c in range(NC):
        cols = slice(c * CW, (c + 1) * CW)
        delta = jnp.dot(packed[...], up[:, cols], preferred_element_type=jnp.float32)
        for e in range(OUT_PER):
            at = slice(e * BLK, (e + 1) * BLK)
            ref_scale, pol_scale = scales[e]
            h = rows[c, sources[e]].astype(jnp.float32)
            reference[at, cols] = (h * ref_scale * gain[:, cols]).astype(jnp.bfloat16)
            policy[at, cols] = ((h + delta[at, :]) * pol_scale * gain[:, cols]).astype(
                jnp.bfloat16
            )


def place(table, rows, inner, lines, adapter_up, gain):
    vector = pl.BlockSpec(memory_space=pltpu.VMEM)
    out_spec = pl.BlockSpec((OUT_PER * BLK, HALF), lambda i, table: (i, 0))
    return pl.pallas_call(
        place_kernel,
        grid_spec=pltpu.PrefetchScalarGridSpec(
            num_scalar_prefetch=1,
            grid=(GROUPS // OUT_PER,),
            in_specs=[vector] * 5,
            out_specs=[out_spec, out_spec],
            scratch_shapes=[pltpu.VMEM((OUT_PER * BLK, RANK), jnp.bfloat16)],
        ),
        out_shape=[jax.ShapeDtypeStruct((ROWS, HALF), jnp.bfloat16)] * 2,
        compiler_params=pltpu.CompilerParams(vmem_limit_bytes=PLACE_LIMIT),
        name="place",
    )(table, rows, inner, lines, adapter_up, gain)


def local(
    context,
    residual,
    out_weight,
    adapter_down,
    adapter_up,
    norm_gain,
    lengths,
    route_group,
    route_slot,
):
    position = jnp.arange(GROUPS, dtype=jnp.int32)
    targets = target(position, lax.axis_index("grp"))
    chosen = route_group[0][None, :] == targets[:, None]
    facts = jnp.stack([position, route_slot[0]])
    meta = jnp.sum(jnp.where(chosen[None], facts[:, None, :], 0), axis=2).astype(jnp.int32)
    rows, inner, lines, table, up = route(
        meta,
        lengths,
        context.reshape(GROUPS, BLK, KDIM),
        residual.reshape(GROUPS, BLK, HALF),
        out_weight,
        adapter_down,
        adapter_up,
    )
    return tuple(place(table[0], rows, inner, lines, up, norm_gain[None, :]))


def solution(mesh):
    in_specs = (
        P("grp", "tp"),
        P("grp", "tp"),
        P("tp", None),
        P("tp", None),
        P(None, "tp"),
        P("tp"),
        P("grp"),
        P("grp", None),
        P("grp", None),
    )
    out_specs = (P("grp", "tp"), P("grp", "tp"))
    return jax.shard_map(local, mesh=mesh, in_specs=in_specs, out_specs=out_specs, check_vma=False)
```

time: 258 us -> 102 us (0.40)
  the two profiles are of different devices: /device:TPU:11 before, /device:TPU:1 now
where the time goes in v2:
time: 102 us; the launch traced here: 101 us
  Pallas kernels  98.6 us (97%)
  other arithmetic  1.52 us (1%)
  between operations  1.32 us (1%)
    pallas_call x1, Pallas kernels, route(): pl.pallas_call(route_kernel, out_shape=(jax.ShapeDtypeStruct((NC, GROUPS,...  90.9 us
    pallas_call x1, Pallas kernels, place(): pl.pallas_call(place_kernel, grid_spec=pltpu.PrefetchScalarGridSpec(num_s...  7.73 us

profile of v2, /device:TPU:1, one launch (start us, length us, event | category | flops | bytes accessed | tf_op | source)
XLA Modules:
  0.0 101.5 jit_solution(18352748667538692200)
XLA Ops:
  1.3 0.7 pad_add_fusion
  2.0 0.7 broadcast_compare_fusion
  2.7 0.1 select_reduce_fusion.meta
  2.8 0.0 copy-start
  2.8 90.9 %route.1 = (bf16[6,64,16,512]{3,2,1,0:T(8,128)(2,1)S(1)}, bf16[64,16,128]{2,1,0:T(8,128)(2,1)S(1)}, f32[64,1,128]{2,1,0:T(1,128)S(1)}, s32[1,128]{1,0:T(1,128)S(1)}, bf16[128,3072]{1,0:T(8,128)(2,1)S(1)}) custom-call(s32[2,64]{1,0:T(2,128)S(1)} %select_reduce_fusion.meta, s32[1]{0:T(128)S(6)} %copy.11.length, bf16[64,16,1536]{2,1,0:T(8,128)(2,1)} %bitcast.9, ...), custom_call_target="tpu_custom_call" | custom-call | flops 19327352832 | bytes 50331648 | tf_op jit(solution)/shard_map/route/pallas_call | solution.py:415
  93.7 0.0 copy-done
  93.7 7.7 %place.1 = (bf16[1024,3072]{1,0:T(8,128)(2,1)}, bf16[1024,3072]{1,0:T(8,128)(2,1)}) custom-call(s32[128]{0:T(128)S(1)} %bitcast.6, bf16[6,64,16,512]{3,2,1,0:T(8,128)(2,1)S(1)} %get-tuple-element.8.refs_0_, bf16[64,16,128]{2,1,0:T(8,128)(2,1)S(1)} %get-tuple-element.9.refs_1_, f32[64,1,128]{2,1,0:T(1,128)S(1)} %get-tuple-element.10.refs_2_, ...), custom_call_target="tpu_custom_call" | custom-call | tf_op jit(solution)/shard_map/place/pallas_call | solution.py:513
  (2 shorter events, 0.0 us)
Async XLA Ops:
  2.8 90.9 %copy-start = (f32[3072]{0:T(1024)S(1)}, f32[3072]{0:T(1024)}, u32[]{:S(2)}) copy-start(f32[3072]{0:T(1024)} %param.14) | copy-start | bytes 36868

commit v3 on v2

--- a/solution.py
+++ b/solution.py
@@ -25,43 +25,12 @@
 NC = HALF // CW
 UNITS = NC * NR
 RING = 4
+HALF_STEPS = GROUPS // 2
 WRING = 4
 
 
-def send_offsets():
-    def distance(o):
-        return sum(min(v, SIDE - v) for v in o)
-
-    def negative(o):
-        return tuple((SIDE - v) % SIDE for v in o)
-
-    every = [(z, y, x) for z in range(SIDE) for y in range(SIDE) for x in range(SIDE)]
-    every.sort(key=distance)
-    alone = [o for o in every if o == negative(o) and o != (0, 0, 0)] + [(0, 0, 0)]
-    pairs = list(zip(alone[::2], alone[1::2]))
-    seen = set(alone)
-    for o in every:
-        if o in seen:
-            continue
-        for turn in (o, (o[1], o[2], o[0]), (o[2], o[0], o[1])):
-            if turn not in seen:
-                pairs.append((turn, negative(turn)))
-                seen.update(pairs[-1])
-    pairs.sort(key=lambda p: 99 if (0, 0, 0) in p else distance(p[0]) + distance(p[1]))
-    return [(z * SIDE + y) * SIDE + x for pair in pairs for z, y, x in pair]
-
-
-def packed_offsets():
-    codes = send_offsets() + [0]
-    return [sum(codes[5 * w + e] << (6 * e) for e in range(5)) for w in range(13)]
-
-
 def target(j, me):
-    word_at = (j * 13) >> 6
-    word = jnp.int32(0)
-    for index, value in enumerate(packed_offsets()):
-        word = jnp.where(word_at == index, jnp.int32(value), word)
-    code = word >> (6 * (j - 5 * word_at))
+    code = ((j + 1) * 27) & 63
     return (
         ((me & 48) + (code & 48)) & 48
         | ((me & 12) + (code & 12)) & 12
@@ -70,7 +39,8 @@
 
 
 def route_kernel(
-    meta,
+    blocks,
+    seats_for,
     length,
     ctx_hbm,
     res_hbm,
@@ -170,16 +140,18 @@
 
     def start_rows(c, j, there):
         far_copy(
-            msg.at[c, j], rows_out.at[c, me], ms_sem.at[c], mr_sem.at[c], there
+            msg.at[c, j], rows_out.at[c, j], ms_sem.at[c], mr_sem.at[c], there
         ).start()
 
-    def inner_copy(j, there, slot):
-        return far_copy(
-            a_full.at[j], inner_out.at[slot], small_sem.at[0], small_sem.at[1], there
-        )
-
-    def line_copy(j, there, slot):
-        return far_copy(line.at[j], lines_out.at[slot], small_sem.at[2], small_sem.at[3], there)
+    def inner_copy(j, there):
+        return far_copy(a_full.at[j], inner_out.at[j], small_sem.at[0], small_sem.at[1], there)
+
+    def line_copy(j, there):
+        return far_copy(line.at[j], lines_out.at[j], small_sem.at[2], small_sem.at[3], there)
+
+    def swap_copy():
+        mine = pl.ds(pl.multiple_of(tp * HALF_STEPS, HALF_STEPS), HALF_STEPS)
+        return mate_copy(inner_out.at[mine], inner_out.at[mine], small_sem.at[4], small_sem.at[5])
 
     loads[0].start()
     loads[1].start()
@@ -199,7 +171,7 @@
     loads[0].wait()
 
     def gather(j, carry):
-        lhs[j] = ctx_v[meta[0, j]]
+        lhs[j] = ctx_v[blocks[j]]
         return carry
 
     lax.fori_loop(0, GROUPS, gather, 0)
@@ -283,10 +255,9 @@
             )
             half_copy(v).wait_recv()
 
-            def finish(i0, c2):
-                i = i0 + tp * (1 - 2 * (i0 % 2))
+            def finish(i, c2):
                 j = r * PER + i
-                block = meta[0, j]
+                block = blocks[j]
                 here = pl.ds(pl.multiple_of(i * BLK, BLK), BLK)
                 h = (
                     own[v % 2, here, :].astype(jnp.float32)
@@ -294,11 +265,6 @@
                     + res_v[block, :, cols].astype(jnp.float32)
                 )
                 msg[c, j] = h.astype(jnp.bfloat16)
-
-                @pl.when(j < GROUPS - 1)
-                def _():
-                    start_rows(c, j, target(j, me))
-
                 q = h + delta[here, :]
                 h2 = h * h
                 q2 = q * q
@@ -311,7 +277,24 @@
                 pol_sq[j] = pol_sum
                 return c2
 
-            lax.fori_loop(0, PER, finish, 0)
+            lax.fori_loop(0, PER, finish, 0, unroll=4)
+            count = PER - r // (NR - 1)
+
+            def post(i, c2):
+                j = r * PER + i
+                start_rows(c, j, target(j, me))
+                return c2
+
+            lax.fori_loop(0, count, post, 0)
+
+            @pl.when((c == 1) & (r // (NR // 2) == tp))
+            def _():
+                def post_inner(i, c2):
+                    j = r * PER + i
+                    inner_copy(j, target(j, me)).start()
+                    return c2
+
+                lax.fori_loop(0, count, post_inner, 0)
 
         return carry
 
@@ -336,7 +319,7 @@
 
         def one(i, c2):
             j = r * PER + i
-            block = meta[0, j]
+            block = blocks[j]
             here = pl.ds(pl.multiple_of(i * BLK, BLK), BLK)
             total = s_send[r, here, :] + s_recv[r, here, :]
             live = jnp.where(block * BLK + token < length[0], 1.0, 0.0)
@@ -347,15 +330,13 @@
                 jnp.where(lane == token + BLK, scale[:, RANK // 2 : RANK // 2 + 1], 0.0),
             )
             seat = jnp.where(
-                (token == 0) & (lane == 2 * BLK), meta[1, j].astype(jnp.float32), 0.0
+                (token == 0) & (lane == 2 * BLK), seats_for[j].astype(jnp.float32), 0.0
             )
             line[j] = jnp.sum(row + seat, axis=0, keepdims=True)
 
             @pl.when(j < GROUPS - 1)
             def _():
-                there = target(j, me)
-                inner_copy(j, there, me).start()
-                line_copy(j, there, me).start()
+                line_copy(j, target(j, me)).start()
 
             return c2
 
@@ -366,13 +347,30 @@
 
     last = GROUPS - 1
     keep = [
-        pltpu.make_async_copy(msg.at[c, last], rows_out.at[c, me], w_sem.at[c])
+        pltpu.make_async_copy(msg.at[c, last], rows_out.at[c, last], w_sem.at[c])
         for c in range(NC)
     ]
-    keep.append(pltpu.make_async_copy(a_full.at[last], inner_out.at[me], load_sem.at[0]))
-    keep.append(pltpu.make_async_copy(line.at[last], lines_out.at[me], load_sem.at[1]))
+    keep.append(pltpu.make_async_copy(line.at[last], lines_out.at[last], load_sem.at[1]))
     for copy in keep:
         copy.start()
+
+    def take_inner(first, count):
+        steps = pl.ds(first, count)
+        for at, ref in enumerate((a_full, inner_out)):
+            pltpu.make_async_copy(ref.at[steps], ref.at[steps], small_sem.at[at]).wait()
+
+    @pl.when(tp == 0)
+    def _():
+        take_inner(0, HALF_STEPS)
+
+    @pl.when(tp == 1)
+    def _():
+        own_inner = pltpu.make_async_copy(a_full.at[last], inner_out.at[last], load_sem.at[0])
+        own_inner.start()
+        take_inner(HALF_STEPS, HALF_STEPS - 1)
+        own_inner.wait()
+
+    swap_copy().start()
 
     def drain_mate(r, carry):
         adapter_copy(r).wait_send()
@@ -390,7 +388,8 @@
         copy.wait()
 
     others = pl.ds(0, last)
-    for at, ref in enumerate((a_full, inner_out, line, lines_out)):
+    swap_copy().wait()
+    for at, ref in ((2, line), (3, lines_out)):
         pltpu.make_async_copy(ref.at[others], ref.at[others], small_sem.at[at]).wait()
     sheet = lines_out[...].reshape(GROUPS, RANK)
     seats = sheet[:, 2 * BLK : 2 * BLK + 1].astype(jnp.int32)
@@ -406,7 +405,7 @@
         pltpu.make_async_copy(came, came, mr_sem.at[c]).wait()
 
 
-def route(meta, length, context, residual, out_weight, adapter_down, adapter_up):
+def route(blocks, seats_for, length, context, residual, out_weight, adapter_down, adapter_up):
     any_space = pl.BlockSpec(memory_space=pl.ANY)
     scalars = pl.BlockSpec(memory_space=pltpu.SMEM)
     vector = pl.BlockSpec(memory_space=pltpu.VMEM)
@@ -421,7 +420,7 @@
             jax.ShapeDtypeStruct((1, RANK), jnp.int32),
             jax.ShapeDtypeStruct((RANK, HALF), bf16),
         ),
-        in_specs=[scalars] * 2 + [any_space] * 5,
+        in_specs=[scalars] * 3 + [any_space] * 5,
         out_specs=(any_space, any_space, vector, vector, vector),
         scratch_shapes=[
             pltpu.VMEM((GROUPS, BLK, KDIM), bf16),
@@ -452,7 +451,7 @@
             dma((NR,)),
             dma((NC,)),
             dma((NC,)),
-            dma((4,)),
+            dma((6,)),
         ],
         compiler_params=pltpu.CompilerParams(
             collective_id=0, has_side_effects=True, vmem_limit_bytes=VMEM_LIMIT
@@ -462,7 +461,8 @@
         ),
         name="route",
     )(
-        meta,
+        blocks,
+        seats_for,
         length,
         *[
             pltpu.with_memory_space_constraint(x, pltpu.HBM)
@@ -473,7 +473,7 @@
 
 VMEM_LIMIT = 44 * 2**20
 PLACE_LIMIT = 24 * 2**20
-OUT_PER = 8
+OUT_PER = 16
 
 
 def place_kernel(table, *refs):
@@ -539,10 +539,11 @@
     position = jnp.arange(GROUPS, dtype=jnp.int32)
     targets = target(position, lax.axis_index("grp"))
     chosen = route_group[0][None, :] == targets[:, None]
-    facts = jnp.stack([position, route_slot[0]])
-    meta = jnp.sum(jnp.where(chosen[None], facts[:, None, :], 0), axis=2).astype(jnp.int32)
+    blocks = jnp.sum(jnp.where(chosen, position[None, :], 0), axis=1).astype(jnp.int32)
+    seats_for = jnp.sum(jnp.where(chosen, route_slot[0][None, :], 0), axis=1).astype(jnp.int32)
     rows, inner, lines, table, up = route(
-        meta,
+        blocks,
+        seats_for,
         lengths,
         context.reshape(GROUPS, BLK, KDIM),
         residual.reshape(GROUPS, BLK, HALF),

time: 102 us -> 98.4 us (0.965)
  Pallas kernels: 98.6 us -> 96 us
    pallas_call x1, Pallas kernels: 90.9 us -> 89.1 us  [route(): pl.pallas_call(route_kernel, out_shape=(jax.ShapeDtypeStruct((NC, GROUPS,...]
where the time goes in v3:
time: 98.4 us; the launch traced here: 98.2 us
  Pallas kernels  96 us (98%)
  between operations  1.31 us (1%)
    pallas_call x1, Pallas kernels, route(): pl.pallas_call(route_kernel, out_shape=(jax.ShapeDtypeStruct((NC, GROUPS,...  89.1 us
    pallas_call x1, Pallas kernels, place(): pl.pallas_call(place_kernel, grid_spec=pltpu.PrefetchScalarGridSpec(num_s...  6.89 us

profile of v3, /device:TPU:1, one launch (start us, length us, event | category | flops | bytes accessed | tf_op | source)
XLA Modules:
  0.0 98.2 jit_solution(6416030379279168432)
XLA Ops:
  1.3 0.8 fusion.1
  2.1 0.0 copy-start
  2.2 89.1 %route.1 = (bf16[6,64,16,512]{3,2,1,0:T(8,128)(2,1)S(1)}, bf16[64,16,128]{2,1,0:T(8,128)(2,1)S(1)}, f32[64,1,128]{2,1,0:T(1,128)S(1)}, s32[1,128]{1,0:T(1,128)S(1)}, bf16[128,3072]{1,0:T(8,128)(2,1)S(1)}) custom-call(s32[64]{0:T(128)S(1)} %get-tuple-element.13.blocks, s32[64]{0:T(128)S(1)} %get-tuple-element.12.seats_for, s32[1]{0:T(128)S(6)} %copy.11.length, ...), custom_call_target="tpu_custom_call" | custom-call | flops 19327352832 | bytes 50331648 | tf_op jit(solution)/shard_map/route/pallas_call | solution.py:414
  91.3 0.0 copy-done
  91.3 6.9 %place.1 = (bf16[1024,3072]{1,0:T(8,128)(2,1)}, bf16[1024,3072]{1,0:T(8,128)(2,1)}) custom-call(s32[128]{0:T(128)S(1)} %bitcast.7, bf16[6,64,16,512]{3,2,1,0:T(8,128)(2,1)S(1)} %get-tuple-element.8.refs_0_, bf16[64,16,128]{2,1,0:T(8,128)(2,1)S(1)} %get-tuple-element.9.refs_1_, f32[64,1,128]{2,1,0:T(1,128)S(1)} %get-tuple-element.10.refs_2_, ...), custom_call_target="tpu_custom_call" | custom-call | tf_op jit(solution)/shard_map/place/pallas_call | solution.py:513
  (1 shorter events, 0.0 us)
Async XLA Ops:
  2.1 89.2 %copy-start = (f32[3072]{0:T(1024)S(1)}, f32[3072]{0:T(1024)}, u32[]{:S(2)}) copy-start(f32[3072]{0:T(1024)} %param.14) | copy-start | bytes 36868

commit v4 on v3

--- a/solution.py
+++ b/solution.py
@@ -159,9 +159,6 @@
     weight_load(0, False).start()
     loads[2].start()
     loads[3].start()
-    for c in range(1, WRING):
-        weight_load(c, True).start()
-        weight_load(c, False).start()
 
     lax.fori_loop(1, GROUPS, greet, 0)
     pl.semaphore_signal(barrier, inc=1, device_id=(me, mate), device_id_type=MESH)
@@ -184,6 +181,8 @@
         )
         return carry
 
+    weight_load(1, True).start()
+    weight_load(1, False).start()
     lax.fori_loop(0, NR, squeeze, 0)
     pl.semaphore_wait(barrier, GROUPS)
 
@@ -242,6 +241,9 @@
             lax.fori_loop(0, NR, adapt, 0)
             loads[2].wait()
             loads[3].wait()
+            for later in range(2, WRING):
+                weight_load(later, True).start()
+                weight_load(later, False).start()
 
         @pl.when(u >= 1)
         def _():

time: 98.4 us -> 96.5 us (0.981)
  Pallas kernels: 96 us -> 94.1 us
    pallas_call x1, Pallas kernels: 89.1 us -> 87.2 us  [route(): pl.pallas_call(route_kernel, out_shape=(jax.ShapeDtypeStruct((NC, GROUPS,...]
where the time goes in v4:
time: 96.5 us; the launch traced here: 96.3 us
  Pallas kernels  94.1 us (98%)
  between operations  1.31 us (1%)
    pallas_call x1, Pallas kernels, route(): pl.pallas_call(route_kernel, out_shape=(jax.ShapeDtypeStruct((NC, GROUPS,...  87.2 us
    pallas_call x1, Pallas kernels, place(): pl.pallas_call(place_kernel, grid_spec=pltpu.PrefetchScalarGridSpec(num_s...  6.89 us

profile of v4, /device:TPU:1, one launch (start us, length us, event | category | flops | bytes accessed | tf_op | source)
XLA Modules:
  0.0 96.3 jit_solution(3525545627706271061)
XLA Ops:
  1.3 0.8 fusion.1
  2.1 0.0 copy-start
  2.2 87.2 %route.1 = (bf16[6,64,16,512]{3,2,1,0:T(8,128)(2,1)S(1)}, bf16[64,16,128]{2,1,0:T(8,128)(2,1)S(1)}, f32[64,1,128]{2,1,0:T(1,128)S(1)}, s32[1,128]{1,0:T(1,128)S(1)}, bf16[128,3072]{1,0:T(8,128)(2,1)S(1)}) custom-call(s32[64]{0:T(128)S(1)} %get-tuple-element.13.blocks, s32[64]{0:T(128)S(1)} %get-tuple-element.12.seats_for, s32[1]{0:T(128)S(6)} %copy.11.length, ...), custom_call_target="tpu_custom_call" | custom-call | flops 19327352832 | bytes 50331648 | tf_op jit(solution)/shard_map/route/pallas_call | solution.py:416
  89.4 0.0 copy-done
  89.4 6.9 %place.1 = (bf16[1024,3072]{1,0:T(8,128)(2,1)}, bf16[1024,3072]{1,0:T(8,128)(2,1)}) custom-call(s32[128]{0:T(128)S(1)} %bitcast.7, bf16[6,64,16,512]{3,2,1,0:T(8,128)(2,1)S(1)} %get-tuple-element.8.refs_0_, bf16[64,16,128]{2,1,0:T(8,128)(2,1)S(1)} %get-tuple-element.9.refs_1_, f32[64,1,128]{2,1,0:T(1,128)S(1)} %get-tuple-element.10.refs_2_, ...), custom_call_target="tpu_custom_call" | custom-call | tf_op jit(solution)/shard_map/place/pallas_call | solution.py:515
  (1 shorter events, 0.0 us)
Async XLA Ops:
  2.1 87.2 %copy-start = (f32[3072]{0:T(1024)S(1)}, f32[3072]{0:T(1024)}, u32[]{:S(2)}) copy-start(f32[3072]{0:T(1024)} %param.14) | copy-start | bytes 36868
